TPU v7x, 32 devices: a whole 2x2x4 slice. The times are simulated.
32 devices in a mesh: dp: 2 (over core), expert: 4 (over y, x), mp: 4 (over z).
Axes of the slice: x: 2, y: 2, z: 4, core: 2. Of those that a mesh axis runs over, the one named last changes fastest.
Arguments:
- hidden_in: bfloat16 [4096, 2048], P(('dp', 'expert')), may hold values from -6 to 6
- norm_gain: float32 [2048], replicated, may hold values from 0.1 to 1.9
- router_w: bfloat16 [2048, 4], replicated, may hold values from -0.0625 to 0.0625
- choices: int32 [4096, 2], P(('dp', 'expert')), may hold values from 0 to 3, all different within a row; in each aligned block of 512 rows (0 to 511, 512 to 1023, ...) at most 384 rows name the same one
- w_gate: bfloat16 [4, 2048, 5632], P('expert', None, 'mp'), may hold values from -0.125 to 0.125
- w_up: bfloat16 [4, 2048, 5632], P('expert', None, 'mp'), may hold values from -0.125 to 0.125
- w_down: bfloat16 [4, 5632, 2048], P('expert', 'mp'), may hold values from -0.109375 to 0.109375
Outputs:
- block_out: bfloat16 [4096, 2048], P(('dp', 'expert'), 'mp')
Inputs may be any that keep to these rules, and one draw needn't show every extreme that they name: `choices`: each row names two different experts. Among the 512 rows of one block of tokens no expert is named more than 384 times, and in every draw some expert is named exactly 384 times in some block.
All inputs are finite; a program needn't handle non-finite values.
Results may differ from a plain program's by a relative error of at most 0.012.
Values may be sent and summed in bfloat16 or wider, within the bound.
A program may use at most 128 MiB of HBM per device.

v0:
```python
import jax
import jax.numpy as jnp
from jax import lax
from jax.sharding import PartitionSpec as P

eps_norm = 1e-06


def pair_slots(choice_ids, expert_count):
    flat_ids = choice_ids.reshape(-1)
    onehot = (flat_ids[:, None] == jnp.arange(expert_count, dtype=jnp.int32)[None, :]).astype(
        jnp.int32
    )
    earlier = jnp.cumsum(onehot, axis=0) - onehot
    slot_ids = jnp.sum(earlier * onehot, axis=1)
    return (flat_ids, slot_ids)


def pair_weights(normed, router_w, choice_ids):
    logits = jnp.dot(normed, router_w, preferred_element_type=jnp.float32)
    picked = jnp.take_along_axis(logits, choice_ids, axis=1)
    first_weight = jax.nn.sigmoid(picked[:, 0] - picked[:, 1])
    return jnp.stack([first_weight, 1.0 - first_weight], axis=1)


def per_device(hidden_in, norm_gain, router_w, choices, w_gate, w_up, w_down):
    experts = lax.axis_size("expert")
    mp_count = lax.axis_size("mp")
    tokens_dev, model_width = hidden_in.shape
    capacity = 3 * tokens_dev // experts
    slice_width = model_width // mp_count
    wide_in = hidden_in.astype(jnp.float32)
    normed = (
        wide_in
        * lax.rsqrt(jnp.mean(wide_in * wide_in, axis=1, keepdims=True) + eps_norm)
        * norm_gain
    ).astype(jnp.bfloat16)
    weights = pair_weights(normed, router_w, choices)
    flat_ids, slot_ids = pair_slots(choices, experts)
    row_index = flat_ids * capacity + slot_ids
    sources = jnp.repeat(normed, 2, axis=0)
    buffer = jnp.zeros((experts * capacity, model_width), jnp.bfloat16).at[row_index].set(sources)
    buffer = buffer.reshape(experts, capacity, model_width)
    column = lax.axis_index("mp") * slice_width
    arrived = lax.all_to_all(buffer, "expert", split_axis=0, concat_axis=0, tiled=True)
    expert_rows = arrived.reshape(experts * capacity, model_width)
    gate_proj = jnp.dot(expert_rows, w_gate[0], preferred_element_type=jnp.float32)
    up_proj = jnp.dot(expert_rows, w_up[0], preferred_element_type=jnp.float32)
    hidden = (jax.nn.silu(gate_proj) * up_proj).astype(jnp.bfloat16)
    partial_value = jnp.dot(hidden, w_down[0], preferred_element_type=jnp.float32).astype(
        jnp.bfloat16
    )
    partial_value = partial_value.reshape(experts, capacity, model_width)
    residual = lax.dynamic_slice_in_dim(wide_in, column, slice_width, 1)
    summed = lax.psum_scatter(
        partial_value.astype(jnp.float32).astype(jnp.bfloat16),
        "mp",
        scatter_dimension=2,
        tiled=True,
    ).astype(jnp.float32)
    returned = lax.all_to_all(
        summed.astype(jnp.bfloat16), "expert", split_axis=0, concat_axis=0, tiled=True
    ).astype(summed.dtype)
    picked = returned.reshape(experts * capacity, slice_width)[row_index].reshape(
        tokens_dev, 2, slice_width
    )
    mixture = jnp.sum(picked * weights[:, :, None], axis=1)
    return (residual + mixture).astype(jnp.bfloat16)


def solution(mesh):
    placed = (
        P(("dp", "expert"), None),
        P(),
        P(),
        P(("dp", "expert"), None),
        P("expert", None, "mp"),
        P("expert", None, "mp"),
        P("expert", "mp", None),
    )
    return jax.shard_map(
        per_device, mesh=mesh, in_specs=placed, out_specs=P(("dp", "expert"), "mp"), check_vma=False
    )
```

profile of v0, /device:TPU:26, one launch (start us, length us, event | category | flops | bytes accessed | tf_op | source)
XLA Modules:
  0.0 311.3 jit_solution(5878964248870109429)
XLA Ops:
  6.5 0.0 copy-start
  6.5 0.0 reduce-scatter.2.cloned.1.call-start
  6.5 0.8 copy.37
  7.4 0.2 eq.29
  7.6 0.2 eq.25
  7.7 0.7 broadcast_multiply_fusion
  8.4 1.1 reduce-window.6
  9.6 0.2 slice_reduce_fusion
  9.8 0.2 reduce-window.9
  10.0 0.1 add_bitcast_fusion
  10.0 0.2 copy.36
  10.2 0.2 mul.59
  10.4 2.1 multiply_reduce_fusion
  12.5 2.2 multiply_convert_fusion
  14.6 0.0 copy-start.3
  14.6 1.3 copy-done.3
  16.0 3.7 %broadcast_in_dim.9 = bf16[512,2,2048]{2,1,0:T(2,128)(2,1)} broadcast(bf16[512,2048]{1,0:T(8,128)(2,1)S(1)} %multiply_convert_fusion), dimensions={0,2} | broadcast | bytes 6291456 | tf_op jit(solution)/shard_map/broadcast_in_dim | solution.py:41
  19.7 7.2 %reshape.115 = bf16[1024,2048]{1,0:T(8,128)(2,1)} reshape(bf16[512,2,2048]{2,1,0:T(2,128)(2,1)} %broadcast_in_dim.9) | data formatting | bytes 8388608 | tf_op jit(solution)/shard_map/reshape | solution.py:41
  26.9 0.0 slice-start
  26.9 11.2 %scatter_custom_fusion = bf16[1536,2048]{1,0:T(8,128)(2,1)} fusion(s32[1024]{0:T(1024)S(1)} %bitcast.49, bf16[1024,2048]{1,0:T(8,128)(2,1)} %reshape.115, bf16[]{:T(256)} %constant.18.clone.1), kind=kCustom, calls=%fused_computation.14 | custom fusion | bytes 6291968 | tf_op jit(solution)/shard_map/scatter | solution.py:42
  38.2 74.2 %all_to_all.10 = bf16[4,384,2048]{2,1,0:T(8,128)(2,1)S(1)} all-to-all(bf16[4,384,2048]{2,1,0:T(8,128)(2,1)} %bitcast.45), channel_id=1, replica_groups=mesh['dp'=2,'expert'=4,'mp'=4] {'expert'}, dimensions={0} | all-to-all | bytes 12582912 | tf_op jit(solution)/shard_map/all_to_all | solution.py:45
  112.4 2.6 copy-done.4
  115.0 0.0 slice-done
  115.0 0.0 slice-done.1
  115.0 12.1 %fusion.6 = f32[1536,1408]{1,0:T(8,128)} fusion(bf16[1536,2048]{1,0:T(8,128)(2,1)S(1)} %bitcast.47, bf16[1,2048,1408]{2,1,0:T(8,128)(2,1)S(1)} %bitcast.54), kind=kOutput, calls=%fused_computation.9 | convolution fusion | flops 8858370048 | bytes 20709376 | tf_op jit(solution)/shard_map/dot_general | solution.py:47
  127.1 28.4 %fusion.2 = bf16[1536,2048]{1,0:T(8,128)(2,1)} fusion(bf16[1536,2048]{1,0:T(8,128)(2,1)} %bitcast.48, f32[1536,1408]{1,0:T(8,128)} %fusion.6, bf16[1,1408,2048]{2,1,0:T(8,128)(2,1)} %param.13, bf16[1,2048,1408]{2,1,0:T(8,128)(2,1)} %param.12), kind=kOutput, calls=%fused_computation.6 | convolution fusion | flops 17732861952 | bytes 32768000 | tf_op jit(solution)/shard_map/dot_general | solution.py:50
  155.4 0.0 reduce-scatter.2.cloned.1.call-update
  155.5 0.0 copy-start.5
  155.5 1.5 copy-done.2
  157.0 2.5 convert_element_type.27
  159.5 106.4 %reduce-scatter.2.cloned.1.call-done = bf16[4,384,512]{2,1,0:T(8,128)(2,1)} async-done(((bf16[4,384,2048]{2,1,0:T(8,128)(2,1)}), bf16[4,384,512]{2,1,0:T(8,128)(2,1)}) %reduce-scatter.2.cloned.1.call-update) | async-done | bytes 1572880 | tf_op jit(solution)/shard_map/reduce_scatter | solution.py:55
  265.9 4.6 %all-to-all-start.1 = ((bf16[4,384,512]{2,1,0:T(8,128)(2,1)}), bf16[4,384,512]{2,1,0:T(8,128)(2,1)}, u32[]{:S(2)}, u32[]{:S(2)}) async-start(bf16[4,384,512]{2,1,0:T(8,128)(2,1)} %reduce-scatter.2.cloned.1.call-done), calls=%async_computation.2 | async-start | bytes 3145728 | tf_op jit(solution)/shard_map/all_to_all | solution.py:61
  270.5 0.0 copy-done.5
  270.5 0.1 copy.39
  270.6 0.2 reshape.105
  270.8 0.0 copy-done
  270.8 2.2 fusion.17
  273.1 9.1 %gather_fusion.1 = f32[1024]{0:T(1024)S(1)} fusion(f32[512,4]{0,1:T(4,128)S(1)} %fusion.17, s32[1024]{0:T(1024)S(1)} %reshape.105), kind=kCustom, calls=%fused_computation.1 | custom fusion | bytes 16384 | tf_op jit(solution)/shard_map/jit(take_along_axis)/gather | solution.py:21
  282.1 0.2 reshape.108
  282.3 0.1 copy.40
  282.5 0.1 copy.41
  282.7 7.1 %all-to-all-done.1 = bf16[4,384,512]{2,1,0:T(8,128)(2,1)} async-done(((bf16[4,384,512]{2,1,0:T(8,128)(2,1)}), bf16[4,384,512]{2,1,0:T(8,128)(2,1)}, u32[]{:S(2)}, u32[]{:S(2)}) %all-to-all-start.1) | async-done | bytes 1572896 | tf_op jit(solution)/shard_map/all_to_all | solution.py:61
  289.8 1.8 bitcast_convert_fusion
  291.6 0.0 copy-start.1
  291.7 4.9 %gather_fusion = f32[1024,512]{1,0:T(8,128)} fusion(f32[1536,512]{1,0:T(8,128)S(1)} %bitcast_convert_fusion, s32[1024]{0:T(1024)S(1)} %broadcast_clamp_fusion), kind=kCustom, calls=%fused_computation | custom fusion | bytes 4198400 | tf_op jit(solution)/shard_map/gather | solution.py:64
  296.6 2.5 reshape.93
  299.1 3.2 %multiply_reduce_fusion.1 = f32[512,512]{1,0:T(8,128)S(1)} fusion(f32[512,2,512]{2,1,0:T(2,128)S(1)} %reshape.93, f32[512,2]{1,0:T(8,128)S(1)} %copy.41), kind=kLoop, calls=%fused_computation.16 | loop fusion | flops 786432 | bytes 3149824 | tf_op jit(solution)/shard_map/reduce_sum | solution.py:67
  302.3 2.2 add_convert_fusion
  (14 shorter events, 0.1 us)
Async XLA Ops:
  6.5 264.3 %copy-start = (bf16[2048,4]{0,1:T(4,128)(2,1)S(1)}, bf16[2048,4]{0,1:T(4,128)(2,1)}, u32[]{:S(2)}) copy-start(bf16[2048,4]{0,1:T(4,128)(2,1)} %param.9) | copy-start | bytes 49156
  6.5 259.3 %reduce-scatter.2.cloned.1.call-start = ((), (), s32[]{:S(2)}) async-start(), calls=%async_computation.3 | async-start | bytes 7864320 | tf_op jit(solution)/shard_map/reduce_scatter | solution.py:55
  14.6 1.3 copy-start.3
  26.9 88.1 %slice-start = ((s8[5767168]{0:T(1024)(128)(4,1)}), s8[1572864]{0:T(1024)(128)(4,1)S(1)}, s32[]{:S(2)}) async-start(s8[5767168]{0:T(1024)(128)(4,1)} %bitcast.53), calls=%async_computation.4 | async-start | bytes 3145728
  38.2 76.8 %slice-start.1 = ((s8[5767168]{0:T(1024)(128)(4,1)}), s8[4194304]{0:T(1024)(128)(4,1)S(1)}, s32[]{:S(2)}) async-start(s8[5767168]{0:T(1024)(128)(4,1)} %bitcast.53), calls=%async_computation.5 | async-start | bytes 8388608
  112.4 2.6 copy-start.4
  155.4 1.6 copy-start.2
  155.5 115.0 %copy-start.5 = (s32[512,2]{0,1:T(2,128)S(1)}, s32[512,2]{0,1:T(2,128)}, u32[]{:S(2)}) copy-start(s32[512,2]{0,1:T(2,128)} %param.10) | copy-start | bytes 12292
  265.9 23.9 %all-to-all-start.1 = ((bf16[4,384,512]{2,1,0:T(8,128)(2,1)}), bf16[4,384,512]{2,1,0:T(8,128)(2,1)}, u32[]{:S(2)}, u32[]{:S(2)}) async-start(bf16[4,384,512]{2,1,0:T(8,128)(2,1)} %reduce-scatter.2.cloned.1.call-done), calls=%async_computation.2 | async-start | bytes 3145728 | tf_op jit(solution)/shard_map/all_to_all | solution.py:61
  291.6 12.8 %copy-start.1 = (bf16[2048,4]{0,1:T(4,128)(2,1)S(1)}, bf16[2048,4]{0,1:T(4,128)(2,1)}, u32[]{:S(2)}) copy-start(bf16[2048,4]{0,1:T(4,128)(2,1)} %param.9) | copy-start | bytes 49156
Sparse Core Ops, SparseCore 0:
  155.6 110.2 reduce-scatter.1
where the time goes:
time: 314 us; the launch traced here: 311 us
  waiting for transfers between devices  114 us (36%)
  blocking collectives  74.2 us (24%)
  local copies, waits for them, and re-layouts  46.6 us (15%)
  matrix products  42.7 us (14%)
  other arithmetic  16.1 us (5%)
  between operations  13.6 us (4%)
  starting transfers between devices  4.61 us (1%)
    reduce_scatter x1, waiting for transfers between devices, per_device(): lax.psum_scatter(partial_value.astype(jnp.float32).astype(jnp.bfloat16),...  106 us
    all_to_all x1, blocking collectives, per_device(): lax.all_to_all(buffer, 'expert', split_axis=0, concat_axis=0, tiled=True)  74.2 us
    dot_general x1, matrix products, per_device(): jnp.dot(hidden, w_down[0], preferred_element_type=jnp.float32)  28.4 us
    dot_general x1, matrix products, per_device(): jnp.dot(expert_rows, w_gate[0], preferred_element_type=jnp.float32)  12.1 us
    scatter x1, local copies, waits for them, and re-layouts, per_device(): jnp.zeros((experts * capacity, model_width), jnp.bfloat16).at[row_index]  11.2 us
    gather x5, local copies, waits for them, and re-layouts, pair_weights(): picked = jnp.take_along_axis(logits, choice_ids, axis=1)  9.69 us
    reshape x1, local copies, waits for them, and re-layouts, per_device(): sources = jnp.repeat(normed, 2, axis=0)  7.22 us
    all_to_all x1, waiting for transfers between devices, per_device(): lax.all_to_all(summed.astype(jnp.bfloat16), 'expert', split_axis=0, conca...  7.12 us
  transfers between devices with their start and end apart: 2, of which 2 were waited for; matrix products, arithmetic and copies ran while one was open for 5% of the time, Pallas kernels for 0%

commit v1 on v0

v1 whole, which is shorter than its diff:
```python
import functools

import jax
import jax.numpy as jnp
from jax import lax
from jax.experimental import pallas as pl
from jax.experimental.pallas import tpu as pltpu
from jax.sharding import PartitionSpec as P

eps_norm = 1e-06
MESH = pl.DeviceIdType.MESH
LANES = 128
TILE = 256
ROWS = 64
f32 = jnp.float32
bf16 = jnp.bfloat16


def xor(a, b, size):
    out, bit = 0, 1
    while bit < size:
        out = out + ((a // bit + b // bit) % 2) * bit
        bit *= 2
    return out


def kernel(
    E, MP, CAP,
    x_ref, gain_ref, router_ref, ch_ref, cht_ref, wg_hbm, wu_hbm, wd_hbm,
    out_ref,
    normed, disp, arr, hid, y, ret, comb, part, zrecv, wg, wu, wd,
    wsem, fs, fr, rs, rr, zs, zr, ls, lr,
):
    T, D = x_ref.shape
    F = wg.shape[1]
    W = D // MP
    HALF = CAP // 2
    far = E - 1
    me = lax.axis_index("expert")
    z = lax.axis_index("mp")
    half = z % 2
    zp = z + 1 - 2 * half

    loads = [
        pltpu.make_async_copy(wg_hbm.at[0], wg, wsem.at[0]),
        pltpu.make_async_copy(wu_hbm.at[0], wu, wsem.at[1]),
        pltpu.make_async_copy(wd_hbm.at[0], wd, wsem.at[2]),
    ]
    for load in loads:
        load.start()

    barrier = pltpu.get_barrier_semaphore()
    for k in range(1, E):
        pl.semaphore_signal(barrier, inc=1, device_id={"expert": xor(me, k, E)}, device_id_type=MESH)
    for d in range(1, MP):
        pl.semaphore_signal(barrier, inc=1, device_id={"mp": (z + d) % MP}, device_id_type=MESH)

    def norm_rows(i, carry):
        rows = pl.ds(pl.multiple_of(i * ROWS, ROWS), ROWS)
        wide = x_ref[rows, :].astype(f32)
        scale = lax.rsqrt(jnp.mean(wide * wide, axis=1, keepdims=True) + eps_norm)
        normed[rows, :] = (wide * scale * gain_ref[...]).astype(bf16)
        return carry

    lax.fori_loop(0, T // ROWS, norm_rows, 0)

    lane = lax.broadcasted_iota(jnp.int32, (T, LANES), 1)
    sub = lax.broadcasted_iota(jnp.int32, (E, T), 0)
    lane_e = jnp.full((T, LANES), -1, jnp.int32)
    sub_e = jnp.full((E, T), -1, jnp.int32)
    for k in range(E):
        lane_e = jnp.where(lane == k, xor(me, k, E), lane_e)
        sub_e = jnp.where(sub == k, xor(me, k, E), sub_e)
    c0, c1 = ch_ref[:, 0:1], ch_ref[:, 1:2]
    is0, is1 = lane_e == c0, lane_e == c1
    any_of = jnp.logical_or(is0, is1)
    any_t = jnp.logical_or(sub_e == cht_ref[0:1, :], sub_e == cht_ref[1:2, :])
    row = lax.broadcasted_iota(jnp.int32, (T, T), 0)
    col = lax.broadcasted_iota(jnp.int32, (T, T), 1)
    lower = (col < row).astype(f32).astype(bf16)
    upper = (row < col).astype(f32).astype(bf16)
    pos = jnp.dot(lower, any_of.astype(f32).astype(bf16), preferred_element_type=f32)
    pos = jnp.where(any_of, pos, -1.0).astype(jnp.int32)
    pos_t = jnp.dot(any_t.astype(f32).astype(bf16), upper, preferred_element_type=f32)
    pos_t = jnp.where(any_t, pos_t, -1.0).astype(jnp.int32)

    slot = lax.broadcasted_iota(jnp.int32, (CAP, T), 0)

    def dispatch(k, dst):
        pick = (slot == pos_t[k : k + 1, :]).astype(f32).astype(bf16)
        for n in range(0, D, 512):
            dst[:, n : n + 512] = jnp.dot(
                pick, normed[:, n : n + 512], preferred_element_type=f32
            ).astype(bf16)

    def forward(k):
        return pltpu.make_async_remote_copy(
            src_ref=disp.at[k - 1], dst_ref=arr.at[k],
            send_sem=fs.at[k], recv_sem=fr.at[k],
            device_id={"expert": xor(me, k, E)}, device_id_type=MESH,
        )

    def rows_of(h):
        return pl.ds(pl.multiple_of(h * HALF, HALF), HALF)

    def forward_far():
        return pltpu.make_async_remote_copy(
            src_ref=disp.at[far - 1, rows_of(half)], dst_ref=arr.at[far, rows_of(half)],
            send_sem=fs.at[far], recv_sem=fr.at[far],
            device_id={"expert": xor(me, far, E)}, device_id_type=MESH,
        )

    def relay():
        return pltpu.make_async_remote_copy(
            src_ref=arr.at[far, rows_of(half)], dst_ref=arr.at[far, rows_of(half)],
            send_sem=ls.at[0], recv_sem=lr.at[0],
            device_id={"mp": zp}, device_id_type=MESH,
        )

    def back(k, m):
        return pltpu.make_async_remote_copy(
            src_ref=y.at[k, m], dst_ref=ret.at[k, m],
            send_sem=rs.at[k, m], recv_sem=rr.at[k, m],
            device_id={"expert": xor(me, k, E)}, device_id_type=MESH,
        )

    def across(d):
        m = (z + d) % MP
        return pltpu.make_async_remote_copy(
            src_ref=part.at[m], dst_ref=zrecv.at[d],
            send_sem=zs.at[d], recv_sem=zr.at[d],
            device_id={"mp": m}, device_id_type=MESH,
        )

    dispatch(far, disp.at[far - 1])
    pl.semaphore_wait(barrier, E - 1 + MP - 1)
    forward_far().start()
    for k in range(1, far):
        dispatch(k, disp.at[k - 1])
        forward(k).start()
    dispatch(0, arr.at[0])

    logits = jnp.dot(normed[...], router_ref[...], preferred_element_type=f32)
    l0 = jnp.sum(jnp.where(lane == c0, logits, 0.0), axis=1, keepdims=True)
    l1 = jnp.sum(jnp.where(lane == c1, logits, 0.0), axis=1, keepdims=True)
    first = jax.nn.sigmoid(l0 - l1)
    place = lax.broadcasted_iota(jnp.int32, (T, CAP), 1)
    for k in range(E):
        e = xor(me, k, E)
        weight = jnp.where(c0 == e, first, 1.0 - first)
        comb[k] = jnp.where(place == pos[:, k : k + 1], weight, 0.0).astype(bf16)

    for load in loads:
        load.wait()

    def ffn(k):
        def tile(cols):
            rows = arr[k]
            gate = jnp.dot(rows, wg[:, cols], preferred_element_type=f32)
            up = jnp.dot(rows, wu[:, cols], preferred_element_type=f32)
            hid[:, cols] = (gate / (1.0 + jnp.exp(-gate)) * up).astype(bf16)

        def step(i, carry):
            tile(pl.ds(pl.multiple_of(i * TILE, TILE), TILE))
            return carry

        lax.fori_loop(0, F // TILE, step, 0)
        if F % TILE:
            tile(pl.ds(F // TILE * TILE, F % TILE))

        def down(j, carry):
            m = (z + 1 + j) % MP
            cols = pl.ds(pl.multiple_of(m * W, W), W)
            y[k, m] = jnp.dot(hid[...], wd[:, cols], preferred_element_type=f32).astype(bf16)

            @pl.when(k > 0)
            def _():
                back(k, m).start()

            return carry

        lax.fori_loop(0, MP, down, 0)

    def block(k, carry):
        @pl.when(jnp.logical_and(k > 0, k < far))
        def _():
            forward(k).wait_recv()

        @pl.when(k == far)
        def _():
            relay().wait_recv()

        ffn(k)

        @pl.when(k == 0)
        def _():
            forward_far().wait_recv()
            relay().start()

        return carry

    lax.fori_loop(0, E, block, 0)

    def mix(m):
        total = jnp.dot(comb[0], y[0, m], preferred_element_type=f32)
        for k in range(1, E):
            back(k, m).wait_recv()
            total = total + jnp.dot(comb[k], ret[k, m], preferred_element_type=f32)
        return total

    def send_chunk(j, carry):
        m = (z + 1 + j) % MP
        part[m] = mix(m).astype(bf16)
        across(1 + j).start()
        return carry

    lax.fori_loop(0, MP - 1, send_chunk, 0)
    cols = pl.ds(pl.multiple_of(z * W, W), W)
    total = x_ref[:, cols].astype(f32) + mix(z)
    for d in range(1, MP):
        across(d).wait_recv()
        total = total + zrecv[d].astype(f32)
    out_ref[...] = total.astype(bf16)

    for k in range(1, far):
        forward(k).wait_send()
    forward_far().wait_send()
    relay().wait_send()

    def drain(k, carry):
        def one(m, c):
            back(k, m).wait_send()
            return c

        return lax.fori_loop(0, MP, one, carry)

    lax.fori_loop(1, E, drain, 0)
    for d in range(1, MP):
        across(d).wait_send()


def per_device(hidden_in, norm_gain, router_w, choices, w_gate, w_up, w_down):
    E = lax.axis_size("expert")
    MP = lax.axis_size("mp")
    T, D = hidden_in.shape
    F = w_gate.shape[2]
    CAP = 3 * T // E
    W = D // MP
    router = jnp.pad(router_w, ((0, 0), (0, LANES - router_w.shape[1])))
    vmem = pl.BlockSpec(memory_space=pltpu.VMEM)
    hbm = pl.BlockSpec(memory_space=pl.ANY)
    dma = pltpu.SemaphoreType.DMA
    rows = E * CAP
    return pl.pallas_call(
        functools.partial(kernel, E, MP, CAP),
        out_shape=jax.ShapeDtypeStruct((T, W), bf16),
        in_specs=[vmem] * 5 + [hbm] * 3,
        out_specs=vmem,
        scratch_shapes=[
            pltpu.VMEM((T, D), bf16),
            pltpu.VMEM((E - 1, CAP, D), bf16),
            pltpu.VMEM((E, CAP, D), bf16),
            pltpu.VMEM((CAP, F), bf16),
            pltpu.VMEM((E, MP, CAP, W), bf16),
            pltpu.VMEM((E, MP, CAP, W), bf16),
            pltpu.VMEM((E, T, CAP), bf16),
            pltpu.VMEM((MP, T, W), bf16),
            pltpu.VMEM((MP, T, W), bf16),
            pltpu.VMEM((D, F), bf16),
            pltpu.VMEM((D, F), bf16),
            pltpu.VMEM((F, D), bf16),
            dma((3,)), dma((E,)), dma((E,)), dma((E, MP)), dma((E, MP)),
            dma((MP,)), dma((MP,)), dma((1,)), dma((1,)),
        ],
        compiler_params=pltpu.CompilerParams(
            collective_id=0, has_side_effects=True, vmem_limit_bytes=62 * 1024 * 1024
        ),
        cost_estimate=pl.CostEstimate(
            flops=6 * rows * D * F, bytes_accessed=6 * D * F, transcendentals=rows * F
        ),
    )(
        hidden_in, norm_gain.reshape(1, D), router, choices, choices.T, w_gate, w_up, w_down
    )


def solution(mesh):
    placed = (
        P(("dp", "expert"), None),
        P(),
        P(),
        P(("dp", "expert"), None),
        P("expert", None, "mp"),
        P("expert", None, "mp"),
        P("expert", "mp", None),
    )
    return jax.shard_map(
        per_device, mesh=mesh, in_specs=placed, out_specs=P(("dp", "expert"), "mp"), check_vma=False
    )
```

time: 314 us -> 163 us (0.52)
  Pallas kernels: 0 us -> 155 us
  waiting for transfers between devices: 114 us -> 0 us
  blocking collectives: 74.2 us -> 0 us
  matrix products: 42.7 us -> 0 us
  local copies, waits for them, and re-layouts: 46.6 us -> 5.34 us
  other arithmetic: 16.1 us -> 0 us
  between operations: 13.6 us -> 0.01 us
  starting transfers between devices: 4.61 us -> 0 us
    pallas_call x0 -> x1, Pallas kernels: none -> 155 us  [per_device(): pl.pallas_call(functools.partial(kernel, E, MP, CAP), out_shape=jax.Shape...]
    reduce_scatter x1 -> x0, waiting for transfers between devices: 106 us -> none  [per_device(): lax.psum_scatter(partial_value.astype(jnp.float32).astype(jnp.bfloat16),...]
    all_to_all x1 -> x0, blocking collectives: 74.2 us -> none  [per_device(): lax.all_to_all(buffer, 'expert', split_axis=0, concat_axis=0, tiled=True)]
    dot_general x3 -> x0, matrix products: 42.7 us -> none  [the longest x1 28.4 us: per_device(): jnp.dot(hidden, w_down[0], preferred_element_type=jnp.float32)]
    gather x6 -> x0, local copies, waits for them, and re-layouts: 14.6 us -> none  [the longest x5 9.69 us: pair_weights(): picked = jnp.take_along_axis(logits, choice_ids, axis=1)]
    scatter x1 -> x0, local copies, waits for them, and re-layouts: 11.2 us -> none  [per_device(): jnp.zeros((experts * capacity, model_width), jnp.bfloat16).at[row_index]]
    reshape x2 -> x0, local copies, waits for them, and re-layouts: 9.71 us -> none  [the longest x1 7.22 us: per_device(): sources = jnp.repeat(normed, 2, axis=0)]
    all_to_all x1 -> x0, waiting for transfers between devices: 7.12 us -> none  [per_device(): lax.all_to_all(summed.astype(jnp.bfloat16), 'expert', split_axis=0, conca...]
  transfers between devices with their start and end apart: 2 -> 0, of which waited for: 2 -> 0; matrix products, arithmetic and copies ran while one was open for 5% -> 0% of each run, Pallas kernels for 0% -> 0%
where the time goes in v1:
time: 163 us; the launch traced here: 160 us
  Pallas kernels  155 us (95%)
  local copies, waits for them, and re-layouts  5.34 us (3%)
    pallas_call x1, Pallas kernels, per_device(): pl.pallas_call(functools.partial(kernel, E, MP, CAP), out_shape=jax.Shape...  155 us
    unnamed x3, local copies, waits for them, and re-layouts  4.43 us

profile of v1, /device:TPU:26, one launch (start us, length us, event | category | flops | bytes accessed | tf_op | source)
XLA Modules:
  0.0 160.1 jit_solution(11174120679766445982)
XLA Ops:
  0.0 1.5 copy.9.ch_ref
  1.5 1.0 copy.8
  2.6 0.9 pad.4.router_ref
  3.5 154.7 %shard_map.73 = bf16[512,512]{1,0:T(8,128)(2,1)} custom-call(bf16[512,2048]{1,0:T(8,128)(2,1)} %x_ref.1, f32[1,2048]{1,0:T(1,128)} %bitcast.3, bf16[2048,128]{1,0:T(8,128)(2,1)} %pad.4.router_ref, s32[512,2]{1,0:T(8,128)} %copy.9.ch_ref, s32[2,512]{1,0:T(2,128)} %bitcast.2, bf16[1,2048,1408]{2,1,0:T(8,128)(2,1)} %wg_hbm.1, bf16[1,2048,1408]{2,1,0:T(8,128)(2,1)} %wu_hbm.1, ...), custom_call_target="tpu_custom_call" | custom-call | flops 26575110144 | bytes 17301504 | tf_op jit(solution)/shard_map/pallas_call | solution.py:254
  158.2 1.9 %copy.11 = bf16[512,512]{1,0:T(8,128)(2,1)} copy(bf16[512,512]{1,0:T(8,128)(2,1)} %shard_map.73) | data formatting | bytes 1048576

commit v2 on v1

--- a/solution.py
+++ b/solution.py
@@ -9,7 +9,6 @@
 
 eps_norm = 1e-06
 MESH = pl.DeviceIdType.MESH
-LANES = 128
 TILE = 256
 ROWS = 64
 f32 = jnp.float32
@@ -26,10 +25,10 @@
 
 def kernel(
     E, MP, CAP,
-    x_ref, gain_ref, router_ref, ch_ref, cht_ref, wg_hbm, wu_hbm, wd_hbm,
+    x_ref, gain_ref, router_ref, ch_ref, wg_hbm, wu_hbm, wd_hbm,
     out_ref,
-    normed, disp, arr, hid, y, ret, comb, part, zrecv, wg, wu, wd,
-    wsem, fs, fr, rs, rr, zs, zr, ls, lr,
+    normed, disp, arr, hid, y, ret, comb, part, zrecv, zy, wg, wu, wd,
+    wsem, fs, fr, rs, rr, zs, zr, ls, lr, ps, pr,
 ):
     T, D = x_ref.shape
     F = wg.shape[1]
@@ -64,25 +63,21 @@
 
     lax.fori_loop(0, T // ROWS, norm_rows, 0)
 
-    lane = lax.broadcasted_iota(jnp.int32, (T, LANES), 1)
     sub = lax.broadcasted_iota(jnp.int32, (E, T), 0)
-    lane_e = jnp.full((T, LANES), -1, jnp.int32)
     sub_e = jnp.full((E, T), -1, jnp.int32)
     for k in range(E):
-        lane_e = jnp.where(lane == k, xor(me, k, E), lane_e)
         sub_e = jnp.where(sub == k, xor(me, k, E), sub_e)
-    c0, c1 = ch_ref[:, 0:1], ch_ref[:, 1:2]
-    is0, is1 = lane_e == c0, lane_e == c1
-    any_of = jnp.logical_or(is0, is1)
-    any_t = jnp.logical_or(sub_e == cht_ref[0:1, :], sub_e == cht_ref[1:2, :])
+    c0, c1 = ch_ref[0:1, :], ch_ref[1:2, :]
+
+    def ones(mask):
+        return jnp.where(mask, 1.0, 0.0).astype(bf16)
+
+    first_t, any_t = ones(sub_e == c0), ones(jnp.logical_or(sub_e == c0, sub_e == c1))
     row = lax.broadcasted_iota(jnp.int32, (T, T), 0)
     col = lax.broadcasted_iota(jnp.int32, (T, T), 1)
-    lower = (col < row).astype(f32).astype(bf16)
-    upper = (row < col).astype(f32).astype(bf16)
-    pos = jnp.dot(lower, any_of.astype(f32).astype(bf16), preferred_element_type=f32)
-    pos = jnp.where(any_of, pos, -1.0).astype(jnp.int32)
-    pos_t = jnp.dot(any_t.astype(f32).astype(bf16), upper, preferred_element_type=f32)
-    pos_t = jnp.where(any_t, pos_t, -1.0).astype(jnp.int32)
+    upper = ones(row < col)
+    pos_t = jnp.dot(any_t, upper, preferred_element_type=f32)
+    pos_t = jnp.where(any_t > 0, pos_t, -1.0).astype(jnp.int32)
 
     slot = lax.broadcasted_iota(jnp.int32, (CAP, T), 0)
 
@@ -124,8 +119,34 @@
             device_id={"expert": xor(me, k, E)}, device_id_type=MESH,
         )
 
-    def across(d):
-        m = (z + d) % MP
+    def back_far(m):
+        return pltpu.make_async_remote_copy(
+            src_ref=y.at[far, m, rows_of(half)], dst_ref=ret.at[far, m, rows_of(half)],
+            send_sem=rs.at[far, m], recv_sem=rr.at[far, m],
+            device_id={"expert": xor(me, far, E)}, device_id_type=MESH,
+        )
+
+    def swap(m):
+        return pltpu.make_async_remote_copy(
+            src_ref=y.at[far, m, rows_of(1 - half)], dst_ref=zy.at[m],
+            send_sem=ps.at[m], recv_sem=pr.at[m],
+            device_id={"mp": zp}, device_id_type=MESH,
+        )
+
+    def pair_sum(m):
+        swap(m).wait_recv()
+        mine = y[far, m, rows_of(half), :].astype(f32)
+        y[far, m, rows_of(half), :] = (mine + zy[m].astype(f32)).astype(bf16)
+        back_far(m).start()
+
+    def chunk(j):
+        other = (2 * (z // 2) + 2 + j) % MP
+        late = j // (MP - 2)
+        last = j // (MP - 1)
+        return other * (1 - late) + (zp * (1 - last) + z * last) * late
+
+    def across(m):
+        d = (m - z + MP) % MP
         return pltpu.make_async_remote_copy(
             src_ref=part.at[m], dst_ref=zrecv.at[d],
             send_sem=zs.at[d], recv_sem=zr.at[d],
@@ -137,23 +158,37 @@
     forward_far().start()
     for k in range(1, far):
         dispatch(k, disp.at[k - 1])
-        forward(k).start()
     dispatch(0, arr.at[0])
 
-    logits = jnp.dot(normed[...], router_ref[...], preferred_element_type=f32)
-    l0 = jnp.sum(jnp.where(lane == c0, logits, 0.0), axis=1, keepdims=True)
-    l1 = jnp.sum(jnp.where(lane == c1, logits, 0.0), axis=1, keepdims=True)
+    def column(left, right):
+        return lax.dot_general(
+            left, right, (((1,), (1,)), ((), ())), preferred_element_type=f32
+        )
+
+    eye = ones(row == col)
+    sub_id = lax.broadcasted_iota(jnp.int32, (E, T), 0)
+    logits = column(normed[...], router_ref[...])
+    l0 = jnp.sum(logits * column(eye, ones(sub_id == c0)), axis=1, keepdims=True)
+    l1 = jnp.sum(logits * column(eye, ones(sub_id == c1)), axis=1, keepdims=True)
     first = jax.nn.sigmoid(l0 - l1)
+    any_of, first_of = column(eye, any_t), column(eye, first_t)
+    pos = column(ones(col < row), any_t)
+    pos = jnp.where(any_of > 0.5, pos, -1.0).astype(jnp.int32)
+    weight = jnp.where(first_of > 0.5, first, 1.0 - first)
     place = lax.broadcasted_iota(jnp.int32, (T, CAP), 1)
     for k in range(E):
-        e = xor(me, k, E)
-        weight = jnp.where(c0 == e, first, 1.0 - first)
-        comb[k] = jnp.where(place == pos[:, k : k + 1], weight, 0.0).astype(bf16)
-
+        comb[k] = jnp.where(place == pos[:, k : k + 1], weight[:, k : k + 1], 0.0).astype(bf16)
+    empty = jnp.zeros((HALF, W), bf16)
+    for m in range(MP):
+        ret[far, m, rows_of(1 - half), :] = empty
+
+    forward_far().wait_send()
+    for k in range(1, far):
+        forward(k).start()
     for load in loads:
         load.wait()
 
-    def ffn(k):
+    def hidden(k):
         def tile(cols):
             rows = arr[k]
             gate = jnp.dot(rows, wg[:, cols], preferred_element_type=f32)
@@ -168,75 +203,78 @@
         if F % TILE:
             tile(pl.ds(F // TILE * TILE, F % TILE))
 
-        def down(j, carry):
-            m = (z + 1 + j) % MP
+    def down(k, after):
+        def step(j, carry):
+            m = chunk(j)
             cols = pl.ds(pl.multiple_of(m * W, W), W)
             y[k, m] = jnp.dot(hid[...], wd[:, cols], preferred_element_type=f32).astype(bf16)
-
-            @pl.when(k > 0)
+            after(m)
+            return carry
+
+        lax.fori_loop(0, MP, step, 0)
+
+    hidden(0)
+    down(0, lambda m: None)
+    forward_far().wait_recv()
+    relay().start()
+    relay().wait_recv()
+    hidden(far)
+    down(far, lambda m: swap(m).start())
+
+    def near(k, carry):
+        forward(k).wait_recv()
+        hidden(k)
+
+        def after(m):
+            back(k, m).start()
+
+            @pl.when(k == 1)
             def _():
-                back(k, m).start()
-
-            return carry
-
-        lax.fori_loop(0, MP, down, 0)
-
-    def block(k, carry):
-        @pl.when(jnp.logical_and(k > 0, k < far))
-        def _():
-            forward(k).wait_recv()
-
-        @pl.when(k == far)
-        def _():
-            relay().wait_recv()
-
-        ffn(k)
-
-        @pl.when(k == 0)
-        def _():
-            forward_far().wait_recv()
-            relay().start()
-
+                pair_sum(m)
+
+        down(k, after)
         return carry
 
-    lax.fori_loop(0, E, block, 0)
+    lax.fori_loop(1, far, near, 0)
 
     def mix(m):
         total = jnp.dot(comb[0], y[0, m], preferred_element_type=f32)
         for k in range(1, E):
-            back(k, m).wait_recv()
+            if k == far:
+                back_far(m).wait_recv()
+            else:
+                back(k, m).wait_recv()
             total = total + jnp.dot(comb[k], ret[k, m], preferred_element_type=f32)
         return total
 
     def send_chunk(j, carry):
-        m = (z + 1 + j) % MP
+        m = chunk(j)
         part[m] = mix(m).astype(bf16)
-        across(1 + j).start()
+        across(m).start()
         return carry
 
     lax.fori_loop(0, MP - 1, send_chunk, 0)
     cols = pl.ds(pl.multiple_of(z * W, W), W)
     total = x_ref[:, cols].astype(f32) + mix(z)
     for d in range(1, MP):
-        across(d).wait_recv()
+        across((z + d) % MP).wait_recv()
         total = total + zrecv[d].astype(f32)
     out_ref[...] = total.astype(bf16)
 
     for k in range(1, far):
         forward(k).wait_send()
-    forward_far().wait_send()
     relay().wait_send()
 
-    def drain(k, carry):
-        def one(m, c):
+    def drain(m, carry):
+        for k in range(1, far):
             back(k, m).wait_send()
-            return c
-
-        return lax.fori_loop(0, MP, one, carry)
-
-    lax.fori_loop(1, E, drain, 0)
+        back_far(m).wait_send()
+        swap(m).wait_send()
+        return carry
+
+    lax.fori_loop(0, MP, drain, 0)
     for d in range(1, MP):
-        across(d).wait_send()
+        across((z + d) % MP).wait_send()
 
 
 def per_device(hidden_in, norm_gain, router_w, choices, w_gate, w_up, w_down):
@@ -246,7 +284,6 @@
     F = w_gate.shape[2]
     CAP = 3 * T // E
     W = D // MP
-    router = jnp.pad(router_w, ((0, 0), (0, LANES - router_w.shape[1])))
     vmem = pl.BlockSpec(memory_space=pltpu.VMEM)
     hbm = pl.BlockSpec(memory_space=pl.ANY)
     dma = pltpu.SemaphoreType.DMA
@@ -254,7 +291,7 @@
     return pl.pallas_call(
         functools.partial(kernel, E, MP, CAP),
         out_shape=jax.ShapeDtypeStruct((T, W), bf16),
-        in_specs=[vmem] * 5 + [hbm] * 3,
+        in_specs=[vmem] * 4 + [hbm] * 3,
         out_specs=vmem,
         scratch_shapes=[
             pltpu.VMEM((T, D), bf16),
@@ -266,11 +303,12 @@
             pltpu.VMEM((E, T, CAP), bf16),
             pltpu.VMEM((MP, T, W), bf16),
             pltpu.VMEM((MP, T, W), bf16),
+            pltpu.VMEM((MP, CAP // 2, W), bf16),
             pltpu.VMEM((D, F), bf16),
             pltpu.VMEM((D, F), bf16),
             pltpu.VMEM((F, D), bf16),
             dma((3,)), dma((E,)), dma((E,)), dma((E, MP)), dma((E, MP)),
-            dma((MP,)), dma((MP,)), dma((1,)), dma((1,)),
+            dma((MP,)), dma((MP,)), dma((1,)), dma((1,)), dma((MP,)), dma((MP,)),
         ],
         compiler_params=pltpu.CompilerParams(
             collective_id=0, has_side_effects=True, vmem_limit_bytes=62 * 1024 * 1024
@@ -279,7 +317,7 @@
             flops=6 * rows * D * F, bytes_accessed=6 * D * F, transcendentals=rows * F
         ),
     )(
-        hidden_in, norm_gain.reshape(1, D), router, choices, choices.T, w_gate, w_up, w_down
+        hidden_in, norm_gain.reshape(1, D), router_w.T, choices.T, w_gate, w_up, w_down
     )
 
 

time: 163 us -> 143 us (0.88); the launches traced: 160 us -> 143 us
  Pallas kernels: 155 us -> 141 us
  local copies, waits for them, and re-layouts: 5.34 us -> 1.87 us
    pallas_call x1, Pallas kernels: 155 us -> 141 us  [per_device(): pl.pallas_call(functools.partial(kernel, E, MP, CAP), out_shape=jax.Shape...]
    unnamed x3 -> x1, local copies, waits for them, and re-layouts: 4.43 us -> 1.87 us
where the time goes in v2:
time: 143 us
  Pallas kernels  141 us (99%)
  local copies, waits for them, and re-layouts  1.87 us (1%)
    pallas_call x1, Pallas kernels, per_device(): pl.pallas_call(functools.partial(kernel, E, MP, CAP), out_shape=jax.Shape...  141 us

profile of v2, /device:TPU:26, one launch (start us, length us, event | category | flops | bytes accessed | tf_op | source)
XLA Modules:
  0.0 143.2 jit_solution(13965203660531373531)
XLA Ops:
  0.0 141.3 %shard_map.73 = bf16[512,512]{1,0:T(8,128)(2,1)} custom-call(bf16[512,2048]{1,0:T(8,128)(2,1)} %x_ref.1, f32[1,2048]{1,0:T(1,128)} %bitcast.4, bf16[4,2048]{1,0:T(4,128)(2,1)} %bitcast.3, s32[2,512]{1,0:T(2,128)} %bitcast.5, bf16[1,2048,1408]{2,1,0:T(8,128)(2,1)} %wg_hbm.1, bf16[1,2048,1408]{2,1,0:T(8,128)(2,1)} %wu_hbm.1, bf16[1,1408,2048]{2,1,0:T(8,128)(2,1)} %wd_hbm.1), custom_call_target="tpu_custom_call" | custom-call | flops 26575110144 | bytes 17301504 | tf_op jit(solution)/shard_map/pallas_call | solution.py:291
  141.3 1.9 %copy.9 = bf16[512,512]{1,0:T(8,128)(2,1)} copy(bf16[512,512]{1,0:T(8,128)(2,1)} %shard_map.73) | data formatting | bytes 1048576

commit v3 on v2

--- a/solution.py
+++ b/solution.py
@@ -11,6 +11,7 @@
 MESH = pl.DeviceIdType.MESH
 TILE = 256
 ROWS = 64
+GROUP = 4
 f32 = jnp.float32
 bf16 = jnp.bfloat16
 
@@ -27,7 +28,7 @@
     E, MP, CAP,
     x_ref, gain_ref, router_ref, ch_ref, wg_hbm, wu_hbm, wd_hbm,
     out_ref,
-    normed, disp, arr, hid, y, ret, comb, part, zrecv, zy, wg, wu, wd,
+    normed, disp, arr, arr_near, hid, y, y_near, ret, comb, part, zrecv, zy, wg, wu, wd,
     wsem, fs, fr, rs, rr, zs, zr, ls, lr, ps, pr,
 ):
     T, D = x_ref.shape
@@ -39,6 +40,8 @@
     z = lax.axis_index("mp")
     half = z % 2
     zp = z + 1 - 2 * half
+    mine = z % GROUP
+    QUARTER = CAP // GROUP
 
     loads = [
         pltpu.make_async_copy(wg_hbm.at[0], wg, wsem.at[0]),
@@ -88,55 +91,62 @@
                 pick, normed[:, n : n + 512], preferred_element_type=f32
             ).astype(bf16)
 
-    def forward(k):
-        return pltpu.make_async_remote_copy(
-            src_ref=disp.at[k - 1], dst_ref=arr.at[k],
-            send_sem=fs.at[k], recv_sem=fr.at[k],
+    def near_rows(k):
+        return pl.ds((k - 1) * HALF, HALF)
+
+    def forward(k, h):
+        return pltpu.make_async_remote_copy(
+            src_ref=disp.at[k - 1, pl.ds(h * HALF, HALF)],
+            dst_ref=arr_near.at[h, near_rows(k)],
+            send_sem=fs.at[k, h], recv_sem=fr.at[k, h],
             device_id={"expert": xor(me, k, E)}, device_id_type=MESH,
         )
 
     def rows_of(h):
         return pl.ds(pl.multiple_of(h * HALF, HALF), HALF)
 
+    own_quarter = pl.ds(pl.multiple_of(mine * QUARTER, QUARTER), QUARTER)
+
     def forward_far():
         return pltpu.make_async_remote_copy(
-            src_ref=disp.at[far - 1, rows_of(half)], dst_ref=arr.at[far, rows_of(half)],
-            send_sem=fs.at[far], recv_sem=fr.at[far],
+            src_ref=disp.at[far - 1, own_quarter], dst_ref=arr.at[1, own_quarter],
+            send_sem=fs.at[far, 0], recv_sem=fr.at[far, 0],
             device_id={"expert": xor(me, far, E)}, device_id_type=MESH,
         )
 
-    def relay():
-        return pltpu.make_async_remote_copy(
-            src_ref=arr.at[far, rows_of(half)], dst_ref=arr.at[far, rows_of(half)],
-            send_sem=ls.at[0], recv_sem=lr.at[0],
-            device_id={"mp": zp}, device_id_type=MESH,
-        )
-
-    def back(k, m):
-        return pltpu.make_async_remote_copy(
-            src_ref=y.at[k, m], dst_ref=ret.at[k, m],
-            send_sem=rs.at[k, m], recv_sem=rr.at[k, m],
+    def relay(d):
+        return pltpu.make_async_remote_copy(
+            src_ref=arr.at[1, own_quarter], dst_ref=arr.at[1, own_quarter],
+            send_sem=ls.at[d], recv_sem=lr.at[d],
+            device_id={"mp": z - mine + (mine + d) % GROUP}, device_id_type=MESH,
+        )
+
+    def back(k, h, m):
+        return pltpu.make_async_remote_copy(
+            src_ref=y_near.at[h, m, near_rows(k)],
+            dst_ref=ret.at[k, m, pl.ds(h * HALF, HALF)],
+            send_sem=rs.at[k, h, m], recv_sem=rr.at[k, h, m],
             device_id={"expert": xor(me, k, E)}, device_id_type=MESH,
         )
 
     def back_far(m):
         return pltpu.make_async_remote_copy(
-            src_ref=y.at[far, m, rows_of(half)], dst_ref=ret.at[far, m, rows_of(half)],
-            send_sem=rs.at[far, m], recv_sem=rr.at[far, m],
+            src_ref=y.at[1, m, rows_of(half)], dst_ref=ret.at[far, m, rows_of(half)],
+            send_sem=rs.at[far, 0, m], recv_sem=rr.at[far, 0, m],
             device_id={"expert": xor(me, far, E)}, device_id_type=MESH,
         )
 
     def swap(m):
         return pltpu.make_async_remote_copy(
-            src_ref=y.at[far, m, rows_of(1 - half)], dst_ref=zy.at[m],
+            src_ref=y.at[1, m, rows_of(1 - half)], dst_ref=zy.at[m],
             send_sem=ps.at[m], recv_sem=pr.at[m],
             device_id={"mp": zp}, device_id_type=MESH,
         )
 
     def pair_sum(m):
         swap(m).wait_recv()
-        mine = y[far, m, rows_of(half), :].astype(f32)
-        y[far, m, rows_of(half), :] = (mine + zy[m].astype(f32)).astype(bf16)
+        kept = y[1, m, rows_of(half), :].astype(f32)
+        y[1, m, rows_of(half), :] = (kept + zy[m].astype(f32)).astype(bf16)
         back_far(m).start()
 
     def chunk(j):
@@ -184,16 +194,19 @@
 
     forward_far().wait_send()
     for k in range(1, far):
-        forward(k).start()
+        forward(k, 0).start()
+    forward_far().wait_recv()
+    for d in range(1, GROUP):
+        relay(d).start()
     for load in loads:
         load.wait()
 
-    def hidden(k):
+    def hidden(source):
         def tile(cols):
-            rows = arr[k]
+            rows = source[...]
             gate = jnp.dot(rows, wg[:, cols], preferred_element_type=f32)
             up = jnp.dot(rows, wu[:, cols], preferred_element_type=f32)
-            hid[:, cols] = (gate / (1.0 + jnp.exp(-gate)) * up).astype(bf16)
+            hid[: rows.shape[0], cols] = (gate / (1.0 + jnp.exp(-gate)) * up).astype(bf16)
 
         def step(i, carry):
             tile(pl.ds(pl.multiple_of(i * TILE, TILE), TILE))
@@ -203,39 +216,42 @@
         if F % TILE:
             tile(pl.ds(F // TILE * TILE, F % TILE))
 
-    def down(k, after):
+    def down(count, target, after):
         def step(j, carry):
             m = chunk(j)
             cols = pl.ds(pl.multiple_of(m * W, W), W)
-            y[k, m] = jnp.dot(hid[...], wd[:, cols], preferred_element_type=f32).astype(bf16)
+            target[m] = jnp.dot(
+                hid[:count, :], wd[:, cols], preferred_element_type=f32
+            ).astype(bf16)
             after(m)
             return carry
 
         lax.fori_loop(0, MP, step, 0)
 
-    hidden(0)
-    down(0, lambda m: None)
-    forward_far().wait_recv()
-    relay().start()
-    relay().wait_recv()
-    hidden(far)
-    down(far, lambda m: swap(m).start())
-
-    def near(k, carry):
-        forward(k).wait_recv()
-        hidden(k)
-
+    def near(h, also):
         def after(m):
-            back(k, m).start()
-
-            @pl.when(k == 1)
-            def _():
-                pair_sum(m)
-
-        down(k, after)
-        return carry
-
-    lax.fori_loop(1, far, near, 0)
+            for k in range(1, far):
+                back(k, h, m).start()
+            also(m)
+
+        hidden(arr_near.at[h])
+        down((E - 2) * HALF, y_near.at[h], after)
+
+    hidden(arr.at[0])
+    down(CAP, y.at[0], lambda m: None)
+    for k in range(1, far):
+        forward(k, 0).wait_send()
+        forward(k, 1).start()
+    for k in range(1, far):
+        forward(k, 0).wait_recv()
+    near(0, lambda m: None)
+    for d in range(1, GROUP):
+        relay(d).wait_recv()
+    hidden(arr.at[1])
+    down(CAP, y.at[1], lambda m: swap(m).start())
+    for k in range(1, far):
+        forward(k, 1).wait_recv()
+    near(1, pair_sum)
 
     def mix(m):
         total = jnp.dot(comb[0], y[0, m], preferred_element_type=f32)
@@ -243,7 +259,8 @@
             if k == far:
                 back_far(m).wait_recv()
             else:
-                back(k, m).wait_recv()
+                back(k, 0, m).wait_recv()
+                back(k, 1, m).wait_recv()
             total = total + jnp.dot(comb[k], ret[k, m], preferred_element_type=f32)
         return total
 
@@ -262,12 +279,14 @@
     out_ref[...] = total.astype(bf16)
 
     for k in range(1, far):
-        forward(k).wait_send()
-    relay().wait_send()
+        forward(k, 1).wait_send()
+    for d in range(1, GROUP):
+        relay(d).wait_send()
 
     def drain(m, carry):
         for k in range(1, far):
-            back(k, m).wait_send()
+            back(k, 0, m).wait_send()
+            back(k, 1, m).wait_send()
         back_far(m).wait_send()
         swap(m).wait_send()
         return carry
@@ -288,6 +307,7 @@
     hbm = pl.BlockSpec(memory_space=pl.ANY)
     dma = pltpu.SemaphoreType.DMA
     rows = E * CAP
+    near_count = (E - 2) * CAP // 2
     return pl.pallas_call(
         functools.partial(kernel, E, MP, CAP),
         out_shape=jax.ShapeDtypeStruct((T, W), bf16),
@@ -296,9 +316,11 @@
         scratch_shapes=[
             pltpu.VMEM((T, D), bf16),
             pltpu.VMEM((E - 1, CAP, D), bf16),
-            pltpu.VMEM((E, CAP, D), bf16),
-            pltpu.VMEM((CAP, F), bf16),
-            pltpu.VMEM((E, MP, CAP, W), bf16),
+            pltpu.VMEM((2, CAP, D), bf16),
+            pltpu.VMEM((2, near_count, D), bf16),
+            pltpu.VMEM((max(CAP, near_count), F), bf16),
+            pltpu.VMEM((2, MP, CAP, W), bf16),
+            pltpu.VMEM((2, MP, near_count, W), bf16),
             pltpu.VMEM((E, MP, CAP, W), bf16),
             pltpu.VMEM((E, T, CAP), bf16),
             pltpu.VMEM((MP, T, W), bf16),
@@ -307,8 +329,8 @@
             pltpu.VMEM((D, F), bf16),
             pltpu.VMEM((D, F), bf16),
             pltpu.VMEM((F, D), bf16),
-            dma((3,)), dma((E,)), dma((E,)), dma((E, MP)), dma((E, MP)),
-            dma((MP,)), dma((MP,)), dma((1,)), dma((1,)), dma((MP,)), dma((MP,)),
+            dma((3,)), dma((E, 2)), dma((E, 2)), dma((E, 2, MP)), dma((E, 2, MP)),
+            dma((MP,)), dma((MP,)), dma((GROUP,)), dma((GROUP,)), dma((MP,)), dma((MP,)),
         ],
         compiler_params=pltpu.CompilerParams(
             collective_id=0, has_side_effects=True, vmem_limit_bytes=62 * 1024 * 1024

time: 143 us -> 127 us (0.89); the launches traced: 143 us -> 126 us
  Pallas kernels: 141 us -> 124 us
    pallas_call x1, Pallas kernels: 141 us -> 124 us  [per_device(): pl.pallas_call(functools.partial(kernel, E, MP, CAP), out_shape=jax.Shape...]
where the time goes in v3:
time: 127 us; the launch traced here: 126 us
  Pallas kernels  124 us (98%)
  local copies, waits for them, and re-layouts  1.87 us (1%)
    pallas_call x1, Pallas kernels, per_device(): pl.pallas_call(functools.partial(kernel, E, MP, CAP), out_shape=jax.Shape...  124 us

profile of v3, /device:TPU:26, one launch (start us, length us, event | category | flops | bytes accessed | tf_op | source)
XLA Modules:
  0.0 125.6 jit_solution(15818059758768492704)
XLA Ops:
  0.0 123.7 %shard_map.73 = bf16[512,512]{1,0:T(8,128)(2,1)} custom-call(bf16[512,2048]{1,0:T(8,128)(2,1)} %x_ref.1, f32[1,2048]{1,0:T(1,128)} %bitcast.4, bf16[4,2048]{1,0:T(4,128)(2,1)} %bitcast.3, s32[2,512]{1,0:T(2,128)} %bitcast.5, bf16[1,2048,1408]{2,1,0:T(8,128)(2,1)} %wg_hbm.1, bf16[1,2048,1408]{2,1,0:T(8,128)(2,1)} %wu_hbm.1, bf16[1,1408,2048]{2,1,0:T(8,128)(2,1)} %wd_hbm.1), custom_call_target="tpu_custom_call" | custom-call | flops 26575110144 | bytes 17301504 | tf_op jit(solution)/shard_map/pallas_call | solution.py:311
  123.7 1.9 %copy.9 = bf16[512,512]{1,0:T(8,128)(2,1)} copy(bf16[512,512]{1,0:T(8,128)(2,1)} %shard_map.73) | data formatting | bytes 1048576

commit v4 on v3

--- a/solution.py
+++ b/solution.py
@@ -82,10 +82,9 @@
     pos_t = jnp.dot(any_t, upper, preferred_element_type=f32)
     pos_t = jnp.where(any_t > 0, pos_t, -1.0).astype(jnp.int32)
 
-    slot = lax.broadcasted_iota(jnp.int32, (CAP, T), 0)
-
-    def dispatch(k, dst):
-        pick = (slot == pos_t[k : k + 1, :]).astype(f32).astype(bf16)
+    def dispatch(k, dst, begin, count):
+        slot = begin + lax.broadcasted_iota(jnp.int32, (count, T), 0)
+        pick = ones(slot == pos_t[k : k + 1, :])
         for n in range(0, D, 512):
             dst[:, n : n + 512] = jnp.dot(
                 pick, normed[:, n : n + 512], preferred_element_type=f32
@@ -150,25 +149,32 @@
         back_far(m).start()
 
     def chunk(j):
-        other = (2 * (z // 2) + 2 + j) % MP
-        late = j // (MP - 2)
-        last = j // (MP - 1)
-        return other * (1 - late) + (zp * (1 - last) + z * last) * late
-
-    def across(m):
-        d = (m - z + MP) % MP
-        return pltpu.make_async_remote_copy(
-            src_ref=part.at[m], dst_ref=zrecv.at[d],
-            send_sem=zs.at[d], recv_sem=zr.at[d],
-            device_id={"mp": m}, device_id_type=MESH,
-        )
-
-    dispatch(far, disp.at[far - 1])
+        return (zp * (1 - j % 2) + z * (j % 2) + 2 * (j // 2 + 1)) % MP
+
+    def far_chunk(j):
+        return (2 * (z // 2) + 2 + j) % MP
+
+    def across(j):
+        return pltpu.make_async_remote_copy(
+            src_ref=part.at[j], dst_ref=zrecv.at[j],
+            send_sem=zs.at[j], recv_sem=zr.at[j],
+            device_id={"mp": zp * (1 - j % 2) + chunk(j) * (j % 2)}, device_id_type=MESH,
+        )
+
+    dispatch(far, disp.at[far - 1, own_quarter], mine * QUARTER, QUARTER)
     pl.semaphore_wait(barrier, E - 1 + MP - 1)
     forward_far().start()
     for k in range(1, far):
-        dispatch(k, disp.at[k - 1])
-    dispatch(0, arr.at[0])
+        dispatch(k, disp.at[k - 1, pl.ds(0, HALF)], 0, HALF)
+    dispatch(0, arr.at[0], 0, CAP)
+    forward_far().wait_send()
+    for k in range(1, far):
+        forward(k, 0).start()
+    forward_far().wait_recv()
+    for d in range(1, GROUP):
+        relay(d).start()
+    for k in range(1, far):
+        dispatch(k, disp.at[k - 1, pl.ds(HALF, HALF)], HALF, HALF)
 
     def column(left, right):
         return lax.dot_general(
@@ -192,16 +198,10 @@
     for m in range(MP):
         ret[far, m, rows_of(1 - half), :] = empty
 
-    forward_far().wait_send()
-    for k in range(1, far):
-        forward(k, 0).start()
-    forward_far().wait_recv()
-    for d in range(1, GROUP):
-        relay(d).start()
     for load in loads:
         load.wait()
 
-    def hidden(source):
+    def hidden(source, also=None):
         def tile(cols):
             rows = source[...]
             gate = jnp.dot(rows, wg[:, cols], preferred_element_type=f32)
@@ -210,48 +210,60 @@
 
         def step(i, carry):
             tile(pl.ds(pl.multiple_of(i * TILE, TILE), TILE))
+            if also is not None:
+                pl.when(i == F // TILE // 2)(also)
             return carry
 
         lax.fori_loop(0, F // TILE, step, 0)
         if F % TILE:
             tile(pl.ds(F // TILE * TILE, F % TILE))
 
-    def down(count, target, after):
+    def down(count, target, order, after):
         def step(j, carry):
-            m = chunk(j)
+            m = order(j)
             cols = pl.ds(pl.multiple_of(m * W, W), W)
             target[m] = jnp.dot(
                 hid[:count, :], wd[:, cols], preferred_element_type=f32
             ).astype(bf16)
-            after(m)
+            after(j, m)
             return carry
 
         lax.fori_loop(0, MP, step, 0)
 
-    def near(h, also):
-        def after(m):
+    def near(h, between, also):
+        def after(j, m):
             for k in range(1, far):
                 back(k, h, m).start()
-            also(m)
-
-        hidden(arr_near.at[h])
-        down((E - 2) * HALF, y_near.at[h], after)
+            also(j)
+
+        between(lambda during: hidden(arr_near.at[h], during))
+        down((E - 2) * HALF, y_near.at[h], chunk, after)
 
     hidden(arr.at[0])
-    down(CAP, y.at[0], lambda m: None)
+    down(CAP, y.at[0], chunk, lambda j, m: None)
     for k in range(1, far):
         forward(k, 0).wait_send()
         forward(k, 1).start()
     for k in range(1, far):
         forward(k, 0).wait_recv()
-    near(0, lambda m: None)
+    near(0, lambda work: work(None), lambda j: None)
     for d in range(1, GROUP):
         relay(d).wait_recv()
     hidden(arr.at[1])
-    down(CAP, y.at[1], lambda m: swap(m).start())
+    down(CAP, y.at[1], far_chunk, lambda j, m: swap(m).start())
     for k in range(1, far):
         forward(k, 1).wait_recv()
-    near(1, pair_sum)
+
+    def first_sums(work):
+        work(lambda: pair_sum(far_chunk(0)))
+        pair_sum(far_chunk(1))
+
+    def later_sums(j):
+        @pl.when(j > 1)
+        def _():
+            pair_sum(far_chunk(j))
+
+    near(1, first_sums, later_sums)
 
     def mix(m):
         total = jnp.dot(comb[0], y[0, m], preferred_element_type=f32)
@@ -264,18 +276,26 @@
             total = total + jnp.dot(comb[k], ret[k, m], preferred_element_type=f32)
         return total
 
-    def send_chunk(j, carry):
-        m = chunk(j)
-        part[m] = mix(m).astype(bf16)
-        across(m).start()
+    def send_chunks(i, carry):
+        even, odd = 2 * i, 2 * i + 1
+        part[even] = mix(chunk(even)).astype(bf16)
+        across(even).start()
+        total = mix(chunk(odd))
+        across(even).wait_recv()
+        part[odd] = (total + zrecv[even].astype(f32)).astype(bf16)
+        across(odd).start()
         return carry
 
-    lax.fori_loop(0, MP - 1, send_chunk, 0)
+    lax.fori_loop(0, MP // 2 - 1, send_chunks, 0)
+    part[MP - 2] = mix(zp).astype(bf16)
+    across(MP - 2).start()
     cols = pl.ds(pl.multiple_of(z * W, W), W)
     total = x_ref[:, cols].astype(f32) + mix(z)
-    for d in range(1, MP):
-        across((z + d) % MP).wait_recv()
-        total = total + zrecv[d].astype(f32)
+    across(MP - 2).wait_recv()
+    total = total + zrecv[MP - 2].astype(f32)
+    for j in range(1, MP - 2, 2):
+        across(j).wait_recv()
+        total = total + zrecv[j].astype(f32)
     out_ref[...] = total.astype(bf16)
 
     for k in range(1, far):
@@ -292,8 +312,8 @@
         return carry
 
     lax.fori_loop(0, MP, drain, 0)
-    for d in range(1, MP):
-        across((z + d) % MP).wait_send()
+    for j in range(MP - 1):
+        across(j).wait_send()
 
 
 def per_device(hidden_in, norm_gain, router_w, choices, w_gate, w_up, w_down):

time: 127 us -> 124 us (0.976)
  Pallas kernels: 124 us -> 120 us
    pallas_call x1, Pallas kernels: 124 us -> 120 us  [per_device(): pl.pallas_call(functools.partial(kernel, E, MP, CAP), out_shape=jax.Shape...]
where the time goes in v4:
time: 124 us; the launch traced here: 122 us
  Pallas kernels  120 us (97%)
  local copies, waits for them, and re-layouts  1.87 us (2%)
    pallas_call x1, Pallas kernels, per_device(): pl.pallas_call(functools.partial(kernel, E, MP, CAP), out_shape=jax.Shape...  120 us

profile of v4, /device:TPU:26, one launch (start us, length us, event | category | flops | bytes accessed | tf_op | source)
XLA Modules:
  0.0 121.9 jit_solution(4177341424494937648)
XLA Ops:
  0.0 120.1 %shard_map.73 = bf16[512,512]{1,0:T(8,128)(2,1)} custom-call(bf16[512,2048]{1,0:T(8,128)(2,1)} %x_ref.1, f32[1,2048]{1,0:T(1,128)} %bitcast.4, bf16[4,2048]{1,0:T(4,128)(2,1)} %bitcast.3, s32[2,512]{1,0:T(2,128)} %bitcast.5, bf16[1,2048,1408]{2,1,0:T(8,128)(2,1)} %wg_hbm.1, bf16[1,2048,1408]{2,1,0:T(8,128)(2,1)} %wu_hbm.1, bf16[1,1408,2048]{2,1,0:T(8,128)(2,1)} %wd_hbm.1), custom_call_target="tpu_custom_call" | custom-call | flops 26575110144 | bytes 17301504 | tf_op jit(solution)/shard_map/pallas_call | solution.py:331
  120.1 1.9 %copy.9 = bf16[512,512]{1,0:T(8,128)(2,1)} copy(bf16[512,512]{1,0:T(8,128)(2,1)} %shard_map.73) | data formatting | bytes 1048576

commit v5 on v4

--- a/solution.py
+++ b/solution.py
@@ -29,7 +29,7 @@
     x_ref, gain_ref, router_ref, ch_ref, wg_hbm, wu_hbm, wd_hbm,
     out_ref,
     normed, disp, arr, arr_near, hid, y, y_near, ret, comb, part, zrecv, zy, wg, wu, wd,
-    wsem, fs, fr, rs, rr, zs, zr, ls, lr, ps, pr,
+    wsem, fs, fr, rs, rr, zs, zr, ls, lr, ps, pr, ns, nr,
 ):
     T, D = x_ref.shape
     F = wg.shape[1]
@@ -93,12 +93,31 @@
     def near_rows(k):
         return pl.ds((k - 1) * HALF, HALF)
 
-    def forward(k, h):
-        return pltpu.make_async_remote_copy(
-            src_ref=disp.at[k - 1, pl.ds(h * HALF, HALF)],
-            dst_ref=arr_near.at[h, near_rows(k)],
-            send_sem=fs.at[k, h], recv_sem=fr.at[k, h],
+    def late_rows(base):
+        return pl.ds(pl.multiple_of(base + half * QUARTER, QUARTER), QUARTER)
+
+    def forward(k):
+        return pltpu.make_async_remote_copy(
+            src_ref=disp.at[k - 1, pl.ds(0, HALF)],
+            dst_ref=arr_near.at[0, near_rows(k)],
+            send_sem=fs.at[k, 0], recv_sem=fr.at[k, 0],
             device_id={"expert": xor(me, k, E)}, device_id_type=MESH,
+        )
+
+    def forward_late(k):
+        return pltpu.make_async_remote_copy(
+            src_ref=disp.at[k - 1, late_rows(HALF)],
+            dst_ref=arr_near.at[1, late_rows((k - 1) * HALF)],
+            send_sem=fs.at[k, 1], recv_sem=fr.at[k, 1],
+            device_id={"expert": xor(me, k, E)}, device_id_type=MESH,
+        )
+
+    def relay_late(k):
+        return pltpu.make_async_remote_copy(
+            src_ref=arr_near.at[1, late_rows((k - 1) * HALF)],
+            dst_ref=arr_near.at[1, late_rows((k - 1) * HALF)],
+            send_sem=ns.at[k], recv_sem=nr.at[k],
+            device_id={"mp": zp}, device_id_type=MESH,
         )
 
     def rows_of(h):
@@ -169,12 +188,12 @@
     dispatch(0, arr.at[0], 0, CAP)
     forward_far().wait_send()
     for k in range(1, far):
-        forward(k, 0).start()
+        forward(k).start()
     forward_far().wait_recv()
     for d in range(1, GROUP):
         relay(d).start()
     for k in range(1, far):
-        dispatch(k, disp.at[k - 1, pl.ds(HALF, HALF)], HALF, HALF)
+        dispatch(k, disp.at[k - 1, late_rows(HALF)], HALF + half * QUARTER, QUARTER)
 
     def column(left, right):
         return lax.dot_general(
@@ -242,17 +261,24 @@
     hidden(arr.at[0])
     down(CAP, y.at[0], chunk, lambda j, m: None)
     for k in range(1, far):
-        forward(k, 0).wait_send()
-        forward(k, 1).start()
-    for k in range(1, far):
-        forward(k, 0).wait_recv()
-    near(0, lambda work: work(None), lambda j: None)
+        forward(k).wait_send()
+        forward_late(k).start()
+    for k in range(1, far):
+        forward(k).wait_recv()
+
+    def pass_late(work):
+        work(None)
+        for k in range(1, far):
+            forward_late(k).wait_recv()
+            relay_late(k).start()
+
+    near(0, pass_late, lambda j: None)
     for d in range(1, GROUP):
         relay(d).wait_recv()
     hidden(arr.at[1])
     down(CAP, y.at[1], far_chunk, lambda j, m: swap(m).start())
     for k in range(1, far):
-        forward(k, 1).wait_recv()
+        relay_late(k).wait_recv()
 
     def first_sums(work):
         work(lambda: pair_sum(far_chunk(0)))
@@ -299,7 +325,8 @@
     out_ref[...] = total.astype(bf16)
 
     for k in range(1, far):
-        forward(k, 1).wait_send()
+        forward_late(k).wait_send()
+        relay_late(k).wait_send()
     for d in range(1, GROUP):
         relay(d).wait_send()
 
@@ -350,7 +377,7 @@
             pltpu.VMEM((D, F), bf16),
             pltpu.VMEM((F, D), bf16),
             dma((3,)), dma((E, 2)), dma((E, 2)), dma((E, 2, MP)), dma((E, 2, MP)),
-            dma((MP,)), dma((MP,)), dma((GROUP,)), dma((GROUP,)), dma((MP,)), dma((MP,)),
+            dma((MP,)), dma((MP,)), dma((GROUP,)), dma((GROUP,)), dma((MP,)), dma((MP,)), dma((E,)), dma((E,)),
         ],
         compiler_params=pltpu.CompilerParams(
             collective_id=0, has_side_effects=True, vmem_limit_bytes=62 * 1024 * 1024

time: 124 us -> 126 us (1.016)
  the two profiles are of different devices: /device:TPU:26 before, /device:TPU:0 now
where the time goes in v5:
time: 126 us
  Pallas kernels  124 us (98%)
  local copies, waits for them, and re-layouts  1.87 us (1%)
    pallas_call x1, Pallas kernels, per_device(): pl.pallas_call(functools.partial(kernel, E, MP, CAP), out_shape=jax.Shape...  124 us

profile of v5, /device:TPU:0, one launch (start us, length us, event | category | flops | bytes accessed | tf_op | source)
XLA Modules:
  0.0 126.3 jit_solution(1054773804530833289)
XLA Ops:
  0.0 124.4 %shard_map.73 = bf16[512,512]{1,0:T(8,128)(2,1)} custom-call(bf16[512,2048]{1,0:T(8,128)(2,1)} %x_ref.1, f32[1,2048]{1,0:T(1,128)} %bitcast.4, bf16[4,2048]{1,0:T(4,128)(2,1)} %bitcast.3, s32[2,512]{1,0:T(2,128)} %bitcast.5, bf16[1,2048,1408]{2,1,0:T(8,128)(2,1)} %wg_hbm.1, bf16[1,2048,1408]{2,1,0:T(8,128)(2,1)} %wu_hbm.1, bf16[1,1408,2048]{2,1,0:T(8,128)(2,1)} %wd_hbm.1), custom_call_target="tpu_custom_call" | custom-call | flops 26575110144 | bytes 17301504 | tf_op jit(solution)/shard_map/pallas_call | solution.py:358
  124.4 1.9 %copy.9 = bf16[512,512]{1,0:T(8,128)(2,1)} copy(bf16[512,512]{1,0:T(8,128)(2,1)} %shard_map.73) | data formatting | bytes 1048576
